TPU v7x, 32 devices: a whole 2x2x4 slice. The times are simulated.
32 devices in a mesh: layer: 2 (over x), row: 4 (over y, core), col: 4 (over z).
Axes of the slice: x: 2, y: 2, z: 4, core: 2. Of those that a mesh axis runs over, the one named last changes fastest.
Arguments:
- leaf_rhs: bfloat16 [2, 4, 4, 1, 256, 1024], P('layer', 'row', 'col'), may hold values from -6 to 6
- leaf_inv: bfloat16 [2, 4, 4, 1, 256, 256], P('layer', 'row', 'col'), may hold values from -0.6 to 1.3, as said below
- leaf_blocks: bfloat16 [2, 4, 4, 16, 256, 256], P('layer', 'row', 'col'), may hold values from -0.1875 to 0.1875
- block_col: int32 [2, 4, 4, 16], P('layer', 'row', 'col'), may hold values from 0 to 3, as said below
- block_row: int32 [2, 4, 4, 16], P('layer', 'row', 'col'), may hold values from 0 to 3, as said below
- block_count: int32 [2, 4, 4], P('layer', 'row', 'col'), may hold values from 2 to 16, as said below
- mid_rhs: bfloat16 [2, 4, 4, 256, 1024], P('layer', 'row', 'col'), may hold values from -6 to 6
- mid_inv: bfloat16 [2, 4, 4, 256, 256], P('layer', 'row', 'col'), may hold values from -0.6 to 1.3, as said below
- anc_blocks: bfloat16 [2, 4, 4, 5, 256, 256], P('layer', 'row', 'col'), may hold values from -0.0625 to 0.0625
- anc_rhs: bfloat16 [5, 256, 1024], replicated, may hold values from -6 to 6
- anc_inv: bfloat16 [5, 256, 256], replicated, may hold values from -0.6 to 1.3, as said below
- anc_lower: bfloat16 [10, 256, 256], replicated, may hold values from -0.25 to 0.25
Outputs:
- leaf_sol: bfloat16 [2, 4, 4, 1, 256, 1024], P('layer', 'row', 'col')
- mid_sol: bfloat16 [2, 4, 4, 256, 1024], P('layer', 'row', 'col')
- anc_sol: bfloat16 [5, 256, 1024], replicated
Inputs may be any that keep to these rules, and one draw needn't show every extreme that they name: Entry n of a device's list names the leaf column, counted over the leaves of the device's grid column with grid rows in order, that block n multiplies; the pairs of block_col and block_row of one device are distinct. `block_row`: entry n names the mid supernode of the device's grid row, by grid column, to whose rows block n adds. The stored blocks of a device are its first block_count entries; later entries and blocks are not used. `leaf_inv`: zero above the diagonal. `mid_inv`: zero above the diagonal. `anc_inv`: zero above the diagonal.
All inputs are finite; a program needn't handle non-finite values.
Results may differ from a plain program's by a relative error of at most 0.013.
Values may be sent and summed in bfloat16 or wider, within the bound.
A program may use at most 64 MiB of HBM per device.

v0:
```python
import functools

import jax
import jax.numpy as jnp
from jax import lax
from jax.experimental import pallas as pl
from jax.experimental.pallas import tpu as pltpu
from jax.sharding import PartitionSpec as P

MESH = pl.DeviceIdType.MESH
LAG = 4


def solve_ancestors(partial_rows, rhs_rows, anc_inv, anc_lower):
    solved = []
    for anc_index in range(anc_inv.shape[0]):
        running = rhs_rows[anc_index].astype(jnp.float32) - partial_rows[anc_index]
        if anc_index > 0:
            offset = anc_index * (anc_index - 1) // 2
            earlier = anc_lower[offset : offset + anc_index]
            running = running - jnp.einsum(
                "bsj,bjt->st", earlier, jnp.stack(solved), preferred_element_type=jnp.float32
            )
        residue = running.astype(jnp.bfloat16)
        solved.append(
            jnp.dot(anc_inv[anc_index], residue, preferred_element_type=jnp.float32).astype(
                jnp.bfloat16
            )
        )
    return jnp.stack(solved)


def add_slots(received):
    return jnp.sum(received, axis=0)


def body(
    leaf_rhs,
    leaf_inv,
    leaf_blocks,
    block_col,
    block_row,
    block_count,
    mid_rhs,
    mid_inv,
    anc_blocks,
    anc_rhs,
    anc_inv,
    anc_lower,
):
    leaf_sol = jnp.einsum(
        "ksj,kjt->kst", leaf_inv[0, 0, 0], leaf_rhs[0, 0, 0], preferred_element_type=jnp.float32
    ).astype(jnp.bfloat16)
    factor_blocks = leaf_blocks[0, 0, 0]
    columns = block_col[0, 0, 0]
    targets = block_row[0, 0, 0]
    live_count = block_count[0, 0, 0]
    grid_cols = lax.axis_size("col")
    empty_term = jnp.zeros((grid_cols,) + leaf_sol.shape[1:], jnp.float32)
    piece = lax.all_gather(leaf_sol, "row", axis=0, tiled=True)
    piece_rows = piece.shape[0]

    def one_block(slot_index, current_sum):
        column = columns[slot_index]
        inside = (column >= 0) & (column < piece_rows)

        def add_one(partial_sum):
            chosen = lax.dynamic_index_in_dim(
                piece, jnp.clip(column, 0, piece_rows - 1), 0, keepdims=False
            )
            product = jnp.dot(factor_blocks[slot_index], chosen, preferred_element_type=jnp.float32)
            row_now = lax.dynamic_index_in_dim(partial_sum, targets[slot_index], 0, keepdims=False)
            return lax.dynamic_update_index_in_dim(
                partial_sum, row_now + product, targets[slot_index], 0
            )

        return lax.cond(inside, add_one, lambda unchanged: unchanged, current_sum)

    mid_terms = lax.fori_loop(0, live_count, one_block, empty_term)
    mid_own = add_slots(lax.all_to_all(mid_terms, "col", split_axis=0, concat_axis=0, tiled=True))
    residue = (mid_rhs[0, 0, 0].astype(jnp.float32) - mid_own).astype(jnp.bfloat16)
    mid_sol = jnp.dot(mid_inv[0, 0, 0], residue, preferred_element_type=jnp.float32).astype(
        jnp.bfloat16
    )
    anc_term = jnp.einsum(
        "asj,jt->ast", anc_blocks[0, 0, 0], mid_sol, preferred_element_type=jnp.float32
    )
    anc_part = lax.psum(anc_term, ("layer", "row", "col"))
    anc_sol = solve_ancestors(anc_part, anc_rhs, anc_inv, anc_lower)
    return (leaf_sol[None, None, None], mid_sol[None, None, None], anc_sol)


def fused_kernel(
    layers,
    rows,
    cols,
    block_col_h,
    block_row_h,
    block_count_h,
    leaf_rhs_h,
    leaf_inv_h,
    blocks_h,
    mid_rhs_h,
    mid_inv_h,
    anc_blocks_h,
    anc_rhs_h,
    anc_inv_h,
    anc_lower_h,
    leaf_out,
    mid_out,
    anc_out,
    block_col,
    block_row,
    block_count,
    leaf_rhs,
    leaf_inv,
    blocks,
    mid_rhs,
    mid_inv,
    anc_rhs,
    anc_inv,
    anc_lower,
    xs,
    dense,
    from_left,
    from_right,
    outgoing,
    acc,
    mid_own,
    mids,
    ancb,
    part_out,
    part_outer,
    part_inner,
    total,
    sol,
    load_sem,
    store_sem,
    a_send,
    a_recv,
    b_send,
    b_recv,
    m_send,
    m_recv,
    g_send,
    g_recv,
    c_send,
    c_recv,
    s_send,
    s_recv,
):
    layer, row, col = (lax.axis_index(name) for name in ("layer", "row", "col"))
    plane = layers * rows
    size, width = mid_own.shape[1:]
    ancestors = sol.shape[0]
    max_blocks = blocks.shape[0]
    half = cols // 2
    sib_row = (row // 2) * 2 + 1 - row % 2
    far_row = (row + rows // 2) % rows
    far_sib_row = (far_row // 2) * 2 + 1 - far_row % 2
    other = (layer + 1) % layers
    sib, across, far = (layer, sib_row, col), (other, row, col), (layer, far_row, col)

    def slot(of_layer, of_row):
        return of_layer * rows + of_row

    me = slot(layer, row)

    def remote(src, dst, send_sem, recv_sem, device):
        return pltpu.make_async_remote_copy(
            src_ref=src,
            dst_ref=dst,
            send_sem=send_sem,
            recv_sem=recv_sem,
            device_id=device,
            device_id_type=MESH,
        )

    def lanes(index):
        return pl.ds(pl.multiple_of(index * width, width), width)

    def depth_of(which):
        return pl.ds(pl.multiple_of(which * size, size), size)

    loads = [
        pltpu.make_async_copy(src, dst, load_sem.at[i])
        for i, (src, dst) in enumerate(
            [
                (leaf_inv_h, leaf_inv),
                (leaf_rhs_h, leaf_rhs),
                (anc_blocks_h, ancb.at[:, :, depth_of(me)]),
                (blocks_h, blocks),
                (mid_rhs_h, mid_rhs),
                (mid_inv_h, mid_inv),
                (anc_rhs_h.at[:, :, lanes(me)], anc_rhs),
                (anc_inv_h, anc_inv),
                (anc_lower_h, anc_lower),
                (block_col_h, block_col),
                (block_row_h, block_row),
                (block_count_h, block_count),
            ]
        )
    ]
    for load in loads:
        load.start()

    barrier = pltpu.get_barrier_semaphore()
    for step in range(1, plane):
        peer = (me + step) % plane
        pl.semaphore_signal(
            barrier, inc=1, device_id=(peer // rows, peer % rows, col), device_id_type=MESH
        )

    @pl.when(col > 0)
    def _():
        pl.semaphore_signal(barrier, inc=1, device_id=(layer, row, col - 1), device_id_type=MESH)

    @pl.when(col < cols - 1)
    def _():
        pl.semaphore_signal(barrier, inc=1, device_id=(layer, row, col + 1), device_id_type=MESH)

    loads[0].wait()
    loads[1].wait()
    ends = (col == 0).astype(jnp.int32) + (col == cols - 1).astype(jnp.int32)
    pl.semaphore_wait(barrier, plane + 1 - ends)

    def leaf_chunk(j, kind):
        at_row = (row, row, far_row)[kind]
        to = (sib, far, sib)[kind]
        ref = xs.at[j, at_row]
        return remote(ref, ref, a_send.at[kind, j], a_recv.at[kind, j], to)

    def leaf_arrival(j, kind):
        at_row = (sib_row, far_row, far_sib_row)[kind]
        ref = xs.at[j, at_row]
        return remote(ref, ref, a_send.at[kind, j], a_recv.at[kind, j], sib)

    def leaf_store(j):
        return pltpu.make_async_copy(
            xs.at[j, row], leaf_out.at[:, lanes(j)], store_sem.at[0, j]
        )

    def leaf_step(j, carry):
        xs[j, row] = jnp.dot(
            leaf_inv[...], leaf_rhs[:, lanes(j)], preferred_element_type=jnp.float32
        ).astype(xs.dtype)
        leaf_chunk(j, 1).start()
        leaf_chunk(j, 0).start()
        leaf_store(j).start()
        return carry

    lax.fori_loop(0, plane, leaf_step, 0)

    def block_copy(kind):
        which = (me, me, me, slot(other, row), slot(layer, far_row), slot(layer, far_row))
        which = (which + (slot(other, far_row),))[kind]
        to = (sib, across, far, sib, sib, across, sib)[kind]
        ref = ancb.at[:, :, depth_of(which)]
        return remote(ref, ref, g_send.at[kind], g_recv.at[kind], to)

    def block_arrival(kind):
        which = (
            slot(layer, sib_row),
            slot(other, row),
            slot(layer, far_row),
            slot(other, sib_row),
            slot(layer, far_sib_row),
            slot(other, far_row),
            slot(other, far_sib_row),
        )[kind]
        ref = ancb.at[:, :, depth_of(which)]
        return remote(ref, ref, g_send.at[kind], g_recv.at[kind], sib)

    loads[2].wait()
    block_copy(1).start()
    block_copy(2).start()
    block_copy(0).start()

    for load in loads[9:] + loads[3:4]:
        load.wait()

    def place_target(m, carry):
        for i in range(rows):
            found = jnp.int32(max_blocks)
            for n in range(max_blocks):
                hit = (block_col[n] == i) & (block_row[n] == m) & (n < block_count[0, 0, 0])
                found = jnp.where(hit, n, found)
            there = found < max_blocks
            block = blocks[jnp.minimum(found, max_blocks - 1)]
            keep = jnp.full(block.shape, there.astype(jnp.int32)) > 0
            dense[m, :, i * size : (i + 1) * size] = jnp.where(
                keep, block.astype(jnp.float32), 0.0
            ).astype(dense.dtype)
        return carry

    lax.fori_loop(0, cols, place_target, 0)

    def gathered(j):
        return xs[j].reshape(rows * size, width)

    def sum_copy(j, m, buffer, to):
        return remote(outgoing.at[j, m], buffer.at[j, m], b_send.at[j, m], b_recv_of(buffer, j, m), to)

    def b_recv_of(buffer, j, m):
        return b_recv.at[0 if buffer is from_left else 1, j, m]

    def sums_on(j, m, buffer, has_more, to):
        outgoing_sum = jnp.dot(dense[m], gathered(j), preferred_element_type=jnp.float32)

        @pl.when(has_more)
        def _():
            sum_copy(j, m, buffer, to).wait_recv()
            outgoing[j, m] = (outgoing_sum + buffer[j, m].astype(jnp.float32)).astype(
                outgoing.dtype
            )

        @pl.when(jnp.logical_not(has_more))
        def _():
            outgoing[j, m] = outgoing_sum.astype(outgoing.dtype)

        sum_copy(j, m, buffer, to).start()

    def mid_copy(j):
        return remote(
            mid_own.at[j], mids.at[me], m_send.at[j], m_recv.at[me], (j // rows, j % rows, col)
        )

    def mid_store(j):
        return pltpu.make_async_copy(mid_own.at[j], mid_out.at[:, lanes(j)], store_sem.at[1, j])

    def forward_leaf(j):
        leaf_arrival(j, 1).wait_recv()
        leaf_chunk(j, 2).start()

    loads[4].wait()
    loads[5].wait()
    forward_leaf(0)

    def sum_step(j, carry):
        @pl.when(j < plane)
        def _():
            @pl.when(j < plane - 1)
            def _():
                forward_leaf(j + 1)

            leaf_arrival(j, 0).wait_recv()
            leaf_arrival(j, 2).wait_recv()
            for distance in range(cols - 1, 0, -1):

                @pl.when(col + distance < cols)
                def _():
                    sums_on(j, col + distance, from_left, col > 0, (layer, row, col + 1))

                @pl.when(col - distance >= 0)
                def _():
                    sums_on(j, col - distance, from_right, col < cols - 1, (layer, row, col - 1))

        @pl.when(j == 3)
        def _():
            block_arrival(1).wait_recv()
            block_copy(3).start()

        @pl.when(j == 6)
        def _():
            block_arrival(2).wait_recv()
            block_copy(5).start()
            block_copy(4).start()

        @pl.when(j >= LAG)
        def _():
            done = j - LAG
            acc[...] = mid_rhs[:, lanes(done)].astype(jnp.float32) - jnp.dot(
                dense[col], gathered(done), preferred_element_type=jnp.float32
            )

            @pl.when(col > 0)
            def _():
                sum_copy(done, col, from_left, sib).wait_recv()
                acc[...] -= from_left[done, col].astype(jnp.float32)

            @pl.when(col < cols - 1)
            def _():
                sum_copy(done, col, from_right, sib).wait_recv()
                acc[...] -= from_right[done, col].astype(jnp.float32)

            solved = jnp.dot(
                mid_inv[...], acc[...].astype(jnp.bfloat16), preferred_element_type=jnp.float32
            ).astype(jnp.bfloat16)
            mid_own[done] = solved

            @pl.when(done == me)
            def _():
                mids[me] = solved

            @pl.when(done != me)
            def _():
                mid_copy(done).start()

            mid_store(done).start()

        return carry

    lax.fori_loop(0, plane + LAG, sum_step, 0)

    block_arrival(5).wait_recv()
    block_copy(6).start()
    for kind in (0, 3, 4, 6):
        block_arrival(kind).wait_recv()
    for step in range(1, plane):
        peer = (me + step) % plane
        remote(mids.at[peer], mids.at[peer], m_send.at[0], m_recv.at[peer], sib).wait_recv()
    for load in loads[6:9]:
        load.wait()

    in_left = col < half
    inward = (layer, row, jnp.where(in_left, col + 1, col - 1))
    outward = (layer, row, jnp.where(in_left, col - 1, col + 1))
    middle = (col == half - 1) | (col == half)
    has_outer = (col > 0) & (col < cols - 1)

    def up_copy(a, buffer, kind, to):
        return remote(part_out.at[a], buffer.at[a], c_send.at[0, a], c_recv.at[kind, a], to)

    def down_copy(a):
        return remote(total.at[a], part_inner.at[a], c_send.at[1, a], c_recv.at[1, a], outward)

    for a in range(ancestors):
        acc[...] = jnp.dot(
            ancb[a], mids[...].reshape(plane * size, width), preferred_element_type=jnp.float32
        )

        @pl.when(has_outer)
        def _():
            up_copy(a, part_outer, 0, sib).wait_recv()
            acc[...] += part_outer[a].astype(jnp.float32)

        part_out[a] = acc[...].astype(part_out.dtype)

        @pl.when(middle)
        def _():
            up_copy(a, part_inner, 1, inward).start()

        @pl.when(jnp.logical_not(middle))
        def _():
            up_copy(a, part_outer, 0, inward).start()

    def sol_ref(a, which):
        return anc_out.at[a, :, lanes(which)]

    def sol_copy(a, kind):
        relay = a % 2
        which = (
            me,
            me,
            me,
            slot(other, row),
            slot(layer, far_row),
            (slot(other, row), slot(layer, far_row))[relay],
            slot(other, far_row),
        )[kind]
        to = (sib, across, far, sib, sib, (far, across)[relay], sib)[kind]
        src = sol.at[a] if kind < 3 else sol_ref(a, which)
        return remote(src, sol_ref(a, which), s_send.at[kind, a], s_recv.at[kind, a], to)

    def sol_arrival(a, kind):
        which = (
            slot(layer, sib_row),
            slot(other, row),
            slot(layer, far_row),
            slot(other, sib_row),
            slot(layer, far_sib_row),
            slot(other, far_row),
            slot(other, far_sib_row),
        )[kind]
        return remote(sol.at[a], sol_ref(a, which), s_send.at[kind, a], s_recv.at[kind, a], sib)

    def sol_store(a):
        return pltpu.make_async_copy(sol.at[a], sol_ref(a, me), store_sem.at[2, a])

    for a in range(ancestors):
        up_copy(a, part_inner, 1, sib).wait_recv()

        @pl.when(middle)
        def _():
            total[a] = (
                part_out[a].astype(jnp.float32) + part_inner[a].astype(jnp.float32)
            ).astype(total.dtype)

        @pl.when(jnp.logical_not(middle))
        def _():
            total[a] = part_inner[a]

        @pl.when(has_outer)
        def _():
            down_copy(a).start()

        running = anc_rhs[a].astype(jnp.float32) - total[a].astype(jnp.float32)
        offset = a * (a - 1) // 2
        for b in range(a):
            running -= jnp.dot(anc_lower[offset + b], sol[b], preferred_element_type=jnp.float32)
        sol[a] = jnp.dot(
            anc_inv[a], running.astype(jnp.bfloat16), preferred_element_type=jnp.float32
        ).astype(sol.dtype)
        for kind in (2, 1, 0):
            sol_copy(a, kind).start()
        sol_store(a).start()

    for a in range(ancestors):
        for kind in ((1, 2), (2, 1))[a % 2]:
            sol_arrival(a, kind).wait_recv()
            if kind == 1 + a % 2:
                sol_copy(a, 5).start()
            sol_copy(a, kind + 2).start()
    for a in range(ancestors):
        sol_arrival(a, 5).wait_recv()
        sol_copy(a, 6).start()

    def drain(j, carry):
        for kind in range(3):
            leaf_chunk(j, kind).wait_send()
        leaf_store(j).wait()
        mid_store(j).wait()

        @pl.when(j != me)
        def _():
            mid_copy(j).wait_send()

        def drain_sums(m, inner):
            @pl.when(m != col)
            def _():
                sum_copy(j, m, from_left, sib).wait_send()

            return inner

        lax.fori_loop(0, cols, drain_sums, 0)
        return carry

    lax.fori_loop(0, plane, drain, 0)
    for kind in range(7):
        block_copy(kind).wait_send()
    for a in range(ancestors):
        up_copy(a, part_inner, 1, sib).wait_send()

        @pl.when(has_outer)
        def _():
            down_copy(a).wait_send()

        for kind in range(7):
            sol_copy(a, kind).wait_send()
        sol_store(a).wait()
        for kind in (0, 3, 4, 6):
            sol_arrival(a, kind).wait_recv()


def place_results(leaf_in, mid_in, anc_in, leaf_out, mid_out, anc_out, sem):
    copies = [
        pltpu.make_async_copy(anc_in.at[a], anc_out.at[a], sem.at[a])
        for a in range(anc_in.shape[0])
    ]
    copies.append(pltpu.make_async_copy(leaf_in, leaf_out, sem.at[len(copies)]))
    copies.append(pltpu.make_async_copy(mid_in, mid_out, sem.at[len(copies)]))
    for copy in copies:
        copy.start()
    for copy in copies:
        copy.wait()


def fused_body(
    layers,
    rows,
    cols,
    leaf_rhs,
    leaf_inv,
    leaf_blocks,
    block_col,
    block_row,
    block_count,
    mid_rhs,
    mid_inv,
    anc_blocks,
    anc_rhs,
    anc_inv,
    anc_lower,
):
    plane = layers * rows
    size, rhs_count = mid_rhs.shape[-2:]
    ancestors = anc_inv.shape[0]
    max_blocks = leaf_blocks.shape[3]
    width = rhs_count // plane
    kept = mid_rhs.dtype
    anywhere = pl.BlockSpec(memory_space=pl.ANY)
    hbm = pl.BlockSpec(memory_space=pltpu.HBM)
    dma = pltpu.SemaphoreType.DMA
    vmem = pltpu.VMEM
    leaf_sol, mid_sol, anc_sol = pl.pallas_call(
        functools.partial(fused_kernel, layers, rows, cols),
        out_shape=[
            jax.ShapeDtypeStruct((size, rhs_count), kept),
            jax.ShapeDtypeStruct((size, rhs_count), kept),
            jax.ShapeDtypeStruct((ancestors, size, rhs_count), kept),
        ],
        in_specs=[hbm] * 12,
        out_specs=[anywhere] * 3,
        scratch_shapes=[
            pltpu.SMEM((max_blocks,), jnp.int32),
            pltpu.SMEM((max_blocks,), jnp.int32),
            pltpu.SMEM(block_count.shape, jnp.int32),
            vmem((size, rhs_count), kept),
            vmem((size, size), kept),
            vmem((max_blocks, size, size), kept),
            vmem((size, rhs_count), kept),
            vmem((size, size), kept),
            vmem((ancestors, size, width), kept),
            vmem(anc_inv.shape, kept),
            vmem(anc_lower.shape, kept),
            vmem((plane, rows, size, width), kept),
            vmem((cols, size, rows * size), kept),
            vmem((plane, cols, size, width), kept),
            vmem((plane, cols, size, width), kept),
            vmem((plane, cols, size, width), kept),
            vmem((size, width), jnp.float32),
            vmem((plane, size, width), kept),
            vmem((plane, size, width), kept),
            vmem((ancestors, size, plane * size), kept),
            vmem((ancestors, size, width), kept),
            vmem((ancestors, size, width), kept),
            vmem((ancestors, size, width), kept),
            vmem((ancestors, size, width), kept),
            vmem((ancestors, size, width), kept),
            dma((12,)),
            dma((3, max(plane, ancestors))),
            dma((3, plane)),
            dma((3, plane)),
            dma((plane, cols)),
            dma((2, plane, cols)),
            dma((plane,)),
            dma((plane,)),
            dma((7,)),
            dma((7,)),
            dma((2, ancestors)),
            dma((2, ancestors)),
            dma((7, ancestors)),
            dma((7, ancestors)),
        ],
        compiler_params=pltpu.CompilerParams(
            collective_id=0, has_side_effects=True, vmem_limit_bytes=62 * 1024 * 1024
        ),
        name="fused_solve",
    )(
        block_col[0, 0, 0],
        block_row[0, 0, 0],
        block_count,
        leaf_rhs[0, 0, 0, 0],
        leaf_inv[0, 0, 0, 0],
        leaf_blocks[0, 0, 0],
        mid_rhs[0, 0, 0],
        mid_inv[0, 0, 0],
        anc_blocks[0, 0, 0],
        anc_rhs,
        anc_inv,
        anc_lower,
    )
    leaf_sol, mid_sol, anc_sol = pl.pallas_call(
        place_results,
        out_shape=[
            jax.ShapeDtypeStruct(value.shape, kept) for value in (leaf_sol, mid_sol, anc_sol)
        ],
        in_specs=[hbm] * 3,
        out_specs=[hbm] * 3,
        scratch_shapes=[dma((2 + ancestors,))],
        compiler_params=pltpu.CompilerParams(vmem_limit_bytes=62 * 1024 * 1024),
        name="place_results",
    )(leaf_sol, mid_sol, anc_sol)
    return (leaf_sol[None, None, None, None], mid_sol[None, None, None], anc_sol)


def fits_fused(mesh, rhs_count):
    layers, rows, cols = (mesh.shape[name] for name in ("layer", "row", "col"))
    pairs = layers == 2 and rows == 4 and cols % 2 == 0
    return pairs and rhs_count % (layers * rows * 128) == 0


def solution(mesh):
    in_specs = (
        P("layer", "row", "col", None, None, None),
        P("layer", "row", "col", None, None, None),
        P("layer", "row", "col", None, None, None),
        P("layer", "row", "col", None),
        P("layer", "row", "col", None),
        P("layer", "row", "col"),
        P("layer", "row", "col", None, None),
        P("layer", "row", "col", None, None),
        P("layer", "row", "col", None, None, None),
        P(),
        P(),
        P(),
    )
    out_specs = (
        P("layer", "row", "col", None, None, None),
        P("layer", "row", "col", None, None),
        P(),
    )

    def run(leaf_rhs, *rest):
        chosen = body
        if fits_fused(mesh, leaf_rhs.shape[-1]) and leaf_rhs.shape[3] == 1:
            sizes = (mesh.shape[name] for name in ("layer", "row", "col"))
            chosen = functools.partial(fused_body, *sizes)
        return jax.shard_map(
            chosen, mesh=mesh, in_specs=in_specs, out_specs=out_specs, check_vma=False
        )(leaf_rhs, *rest)

    return run
```

profile of v0, /device:TPU:0, one launch (start us, length us, event | category | flops | bytes accessed | tf_op | source)
XLA Modules:
  0.0 202.4 jit_solution(1874135321006201593)
XLA Ops:
  1.3 88.8 %fused_solve.1 = (bf16[256,1024]{1,0:T(8,128)(2,1)}, bf16[256,1024]{1,0:T(8,128)(2,1)}, bf16[5,256,1024]{2,1,0:T(8,128)(2,1)}) custom-call(s32[16]{0:T(128)} %bitcast.16, s32[16]{0:T(128)} %bitcast.17, s32[1,1,1]{2,1,0:T(1,128)S(6)} %copy.15.block_count_h, bf16[256,1024]{1,0:T(8,128)(2,1)} %bitcast.12, bf16[256,256]{1,0:T(8,128)(2,1)} %bitcast.14, ...), custom_call_target="tpu_custom_call" | custom-call | tf_op jit(solution)/shard_map/fused_solve/pallas_call | solution.py:595
  90.1 112.3 %place_results.1 = (bf16[256,1024]{1,0:T(8,128)(2,1)}, bf16[256,1024]{1,0:T(8,128)(2,1)}, bf16[5,256,1024]{2,1,0:T(8,128)(2,1)}) custom-call(bf16[256,1024]{1,0:T(8,128)(2,1)} %get-tuple-element.9.leaf_in, bf16[256,1024]{1,0:T(8,128)(2,1)} %get-tuple-element.10.mid_in, bf16[5,256,1024]{2,1,0:T(8,128)(2,1)} %get-tuple-element.11.anc_in), custom_call_target="tpu_custom_call" | custom-call | tf_op jit(solution)/shard_map/place_results/pallas_call | solution.py:663
where the time goes:
time: 203 us; the launch traced here: 202 us
  Pallas kernels  201 us (99%)
    pallas_call x1, Pallas kernels, fused_body(): pl.pallas_call(place_results, out_shape=[jax.ShapeDtypeStruct(value.shape...  112 us
    pallas_call x1, Pallas kernels, fused_body(): pl.pallas_call(functools.partial(fused_kernel, layers, rows, cols), out_s...  88.8 us

commit v1 on v0

--- a/solution.py
+++ b/solution.py
@@ -424,7 +424,7 @@
     def down_copy(a):
         return remote(total.at[a], part_inner.at[a], c_send.at[1, a], c_recv.at[1, a], outward)
 
-    for a in range(ancestors):
+    def sum_up(a):
         acc[...] = jnp.dot(
             ancb[a], mids[...].reshape(plane * size, width), preferred_element_type=jnp.float32
         )
@@ -448,17 +448,17 @@
         return anc_out.at[a, :, lanes(which)]
 
     def sol_copy(a, kind):
-        relay = a % 2
+        turn = a % 2
         which = (
             me,
             me,
             me,
             slot(other, row),
             slot(layer, far_row),
-            (slot(other, row), slot(layer, far_row))[relay],
+            (slot(other, row), slot(layer, far_row))[turn],
             slot(other, far_row),
         )[kind]
-        to = (sib, across, far, sib, sib, (far, across)[relay], sib)[kind]
+        to = (sib, across, far, sib, sib, (far, across)[turn], sib)[kind]
         src = sol.at[a] if kind < 3 else sol_ref(a, which)
         return remote(src, sol_ref(a, which), s_send.at[kind, a], s_recv.at[kind, a], to)
 
@@ -477,7 +477,7 @@
     def sol_store(a):
         return pltpu.make_async_copy(sol.at[a], sol_ref(a, me), store_sem.at[2, a])
 
-    for a in range(ancestors):
+    def solve_down(a):
         up_copy(a, part_inner, 1, sib).wait_recv()
 
         @pl.when(middle)
@@ -505,12 +505,19 @@
             sol_copy(a, kind).start()
         sol_store(a).start()
 
-    for a in range(ancestors):
+    def relay(a):
         for kind in ((1, 2), (2, 1))[a % 2]:
             sol_arrival(a, kind).wait_recv()
             if kind == 1 + a % 2:
                 sol_copy(a, 5).start()
             sol_copy(a, kind + 2).start()
+    for a in range(ancestors + 3):
+        if a < ancestors:
+            sum_up(a)
+        if 2 <= a < ancestors + 2:
+            solve_down(a - 2)
+        if a >= 3:
+            relay(a - 3)
     for a in range(ancestors):
         sol_arrival(a, 5).wait_recv()
         sol_copy(a, 6).start()
@@ -552,17 +559,20 @@
             sol_arrival(a, kind).wait_recv()
 
 
-def place_results(leaf_in, mid_in, anc_in, leaf_out, mid_out, anc_out, sem):
-    copies = [
-        pltpu.make_async_copy(anc_in.at[a], anc_out.at[a], sem.at[a])
-        for a in range(anc_in.shape[0])
-    ]
-    copies.append(pltpu.make_async_copy(leaf_in, leaf_out, sem.at[len(copies)]))
-    copies.append(pltpu.make_async_copy(mid_in, mid_out, sem.at[len(copies)]))
-    for copy in copies:
-        copy.start()
-    for copy in copies:
-        copy.wait()
+def place_results(leaf_in, mid_in, anc_in, leaf_out, mid_out, anc_out, held, anc_held, sem):
+    ancestors = anc_in.shape[0]
+    parts = [(anc_in.at[a], anc_held.at[a], anc_out.at[a]) for a in range(ancestors)]
+    parts.append((leaf_in, held.at[0], leaf_out))
+    parts.append((mid_in, held.at[1], mid_out))
+    reads = [pltpu.make_async_copy(a, b, sem.at[0, i]) for i, (a, b, _) in enumerate(parts)]
+    writes = [pltpu.make_async_copy(b, c, sem.at[1, i]) for i, (_, b, c) in enumerate(parts)]
+    for read in reads:
+        read.start()
+    for read, write in zip(reads, writes):
+        read.wait()
+        write.start()
+    for write in writes:
+        write.wait()
 
 
 def fused_body(
@@ -667,7 +677,11 @@
         ],
         in_specs=[hbm] * 3,
         out_specs=[hbm] * 3,
-        scratch_shapes=[dma((2 + ancestors,))],
+        scratch_shapes=[
+            vmem((2, size, rhs_count), kept),
+            vmem(anc_sol.shape, kept),
+            dma((2, 2 + ancestors)),
+        ],
         compiler_params=pltpu.CompilerParams(vmem_limit_bytes=62 * 1024 * 1024),
         name="place_results",
     )(leaf_sol, mid_sol, anc_sol)

time: 203 us -> 104 us (0.51)
  Pallas kernels: 201 us -> 103 us
    pallas_call x1, Pallas kernels: 112 us -> 3.02 us  [fused_body(): pl.pallas_call(place_results, out_shape=[jax.ShapeDtypeStruct(value.shape...]
    pallas_call x1, Pallas kernels: 88.8 us -> 100 us  [fused_body(): pl.pallas_call(functools.partial(fused_kernel, layers, rows, cols), out_s...]
where the time goes in v1:
time: 104 us
  Pallas kernels  103 us (99%)
  between operations  1.29 us (1%)
    pallas_call x1, Pallas kernels, fused_body(): pl.pallas_call(functools.partial(fused_kernel, layers, rows, cols), out_s...  100 us
    pallas_call x1, Pallas kernels, fused_body(): pl.pallas_call(place_results, out_shape=[jax.ShapeDtypeStruct(value.shape...  3.02 us

profile of v1, /device:TPU:0, one launch (start us, length us, event | category | flops | bytes accessed | tf_op | source)
XLA Modules:
  0.0 104.3 jit_solution(9538083857207607486)
XLA Ops:
  1.3 100.0 %fused_solve.1 = (bf16[256,1024]{1,0:T(8,128)(2,1)}, bf16[256,1024]{1,0:T(8,128)(2,1)}, bf16[5,256,1024]{2,1,0:T(8,128)(2,1)}) custom-call(s32[16]{0:T(128)} %bitcast.16, s32[16]{0:T(128)} %bitcast.17, s32[1,1,1]{2,1,0:T(1,128)S(6)} %copy.15.block_count_h, bf16[256,1024]{1,0:T(8,128)(2,1)} %bitcast.12, bf16[256,256]{1,0:T(8,128)(2,1)} %bitcast.14, ...), custom_call_target="tpu_custom_call" | custom-call | tf_op jit(solution)/shard_map/fused_solve/pallas_call | solution.py:605
  101.2 3.0 %place_results.1 = (bf16[256,1024]{1,0:T(8,128)(2,1)}, bf16[256,1024]{1,0:T(8,128)(2,1)}, bf16[5,256,1024]{2,1,0:T(8,128)(2,1)}) custom-call(bf16[256,1024]{1,0:T(8,128)(2,1)} %get-tuple-element.9.leaf_in, bf16[256,1024]{1,0:T(8,128)(2,1)} %get-tuple-element.10.mid_in, bf16[5,256,1024]{2,1,0:T(8,128)(2,1)} %get-tuple-element.11.anc_in), custom_call_target="tpu_custom_call" | custom-call | tf_op jit(solution)/shard_map/place_results/pallas_call | solution.py:673

commit v2 on v1

--- a/solution.py
+++ b/solution.py
@@ -8,7 +8,7 @@
 from jax.sharding import PartitionSpec as P
 
 MESH = pl.DeviceIdType.MESH
-LAG = 4
+LAG_END, LAG_INSIDE = 7, 3
 
 
 def solve_ancestors(partial_rows, rhs_rows, anc_inv, anc_lower):
@@ -126,6 +126,8 @@
     from_right,
     outgoing,
     acc,
+    terms,
+    own_terms,
     mid_own,
     mids,
     ancb,
@@ -305,7 +307,7 @@
         return b_recv.at[0 if buffer is from_left else 1, j, m]
 
     def sums_on(j, m, buffer, has_more, to):
-        outgoing_sum = jnp.dot(dense[m], gathered(j), preferred_element_type=jnp.float32)
+        outgoing_sum = terms[m]
 
         @pl.when(has_more)
         def _():
@@ -335,6 +337,7 @@
     loads[4].wait()
     loads[5].wait()
     forward_leaf(0)
+    lag = jnp.where((col == 0) | (col == cols - 1), LAG_END, LAG_INSIDE)
 
     def sum_step(j, carry):
         @pl.when(j < plane)
@@ -345,6 +348,12 @@
 
             leaf_arrival(j, 0).wait_recv()
             leaf_arrival(j, 2).wait_recv()
+            terms[...] = jnp.dot(
+                dense[...].reshape(cols * size, rows * size),
+                gathered(j),
+                preferred_element_type=jnp.float32,
+            ).reshape(cols, size, width)
+            own_terms[j] = terms[col]
             for distance in range(cols - 1, 0, -1):
 
                 @pl.when(col + distance < cols)
@@ -366,12 +375,10 @@
             block_copy(5).start()
             block_copy(4).start()
 
-        @pl.when(j >= LAG)
-        def _():
-            done = j - LAG
-            acc[...] = mid_rhs[:, lanes(done)].astype(jnp.float32) - jnp.dot(
-                dense[col], gathered(done), preferred_element_type=jnp.float32
-            )
+        @pl.when((j >= lag) & (j < plane + lag))
+        def _():
+            done = j - lag
+            acc[...] = mid_rhs[:, lanes(done)].astype(jnp.float32) - own_terms[done]
 
             @pl.when(col > 0)
             def _():
@@ -400,7 +407,7 @@
 
         return carry
 
-    lax.fori_loop(0, plane + LAG, sum_step, 0)
+    lax.fori_loop(0, plane + max(LAG_END, LAG_INSIDE), sum_step, 0)
 
     block_arrival(5).wait_recv()
     block_copy(6).start()
@@ -477,23 +484,20 @@
     def sol_store(a):
         return pltpu.make_async_copy(sol.at[a], sol_ref(a, me), store_sem.at[2, a])
 
-    def solve_down(a):
-        up_copy(a, part_inner, 1, sib).wait_recv()
-
-        @pl.when(middle)
-        def _():
-            total[a] = (
-                part_out[a].astype(jnp.float32) + part_inner[a].astype(jnp.float32)
-            ).astype(total.dtype)
-
-        @pl.when(jnp.logical_not(middle))
-        def _():
-            total[a] = part_inner[a]
-
-        @pl.when(has_outer)
-        def _():
-            down_copy(a).start()
-
+    def total_down(a, of_middle):
+        @pl.when(middle if of_middle else jnp.logical_not(middle))
+        def _():
+            up_copy(a, part_inner, 1, sib).wait_recv()
+            value = part_inner[a].astype(jnp.float32)
+            if of_middle:
+                value += part_out[a].astype(jnp.float32)
+            total[a] = value.astype(total.dtype)
+
+            @pl.when(has_outer)
+            def _():
+                down_copy(a).start()
+
+    def solve(a):
         running = anc_rhs[a].astype(jnp.float32) - total[a].astype(jnp.float32)
         offset = a * (a - 1) // 2
         for b in range(a):
@@ -511,13 +515,16 @@
             if kind == 1 + a % 2:
                 sol_copy(a, 5).start()
             sol_copy(a, kind + 2).start()
-    for a in range(ancestors + 3):
+    for a in range(ancestors + 2):
         if a < ancestors:
             sum_up(a)
-        if 2 <= a < ancestors + 2:
-            solve_down(a - 2)
-        if a >= 3:
-            relay(a - 3)
+        if a >= 2:
+            total_down(a - 2, True)
+    for a in range(ancestors):
+        total_down(a, False)
+        solve(a)
+    for a in range(ancestors):
+        relay(a)
     for a in range(ancestors):
         sol_arrival(a, 5).wait_recv()
         sol_copy(a, 6).start()
@@ -629,6 +636,8 @@
             vmem((plane, cols, size, width), kept),
             vmem((plane, cols, size, width), kept),
             vmem((size, width), jnp.float32),
+            vmem((cols, size, width), jnp.float32),
+            vmem((plane, size, width), jnp.float32),
             vmem((plane, size, width), kept),
             vmem((plane, size, width), kept),
             vmem((ancestors, size, plane * size), kept),

time: 104 us -> 94.3 us (0.907)
  Pallas kernels: 103 us -> 92.8 us
    pallas_call x1, Pallas kernels: 100 us -> 89.8 us  [fused_body(): pl.pallas_call(functools.partial(fused_kernel, layers, rows, cols), out_s...]
where the time goes in v2:
time: 94.3 us; the launch traced here: 94.1 us
  Pallas kernels  92.8 us (98%)
  between operations  1.29 us (1%)
    pallas_call x1, Pallas kernels, fused_body(): pl.pallas_call(functools.partial(fused_kernel, layers, rows, cols), out_s...  89.8 us
    pallas_call x1, Pallas kernels, fused_body(): pl.pallas_call(place_results, out_shape=[jax.ShapeDtypeStruct(value.shape...  3.02 us

profile of v2, /device:TPU:0, one launch (start us, length us, event | category | flops | bytes accessed | tf_op | source)
XLA Modules:
  0.0 94.1 jit_solution(1971655557573369105)
XLA Ops:
  1.3 89.8 %fused_solve.1 = (bf16[256,1024]{1,0:T(8,128)(2,1)}, bf16[256,1024]{1,0:T(8,128)(2,1)}, bf16[5,256,1024]{2,1,0:T(8,128)(2,1)}) custom-call(s32[16]{0:T(128)} %bitcast.16, s32[16]{0:T(128)} %bitcast.17, s32[1,1,1]{2,1,0:T(1,128)S(6)} %copy.15.block_count_h, bf16[256,1024]{1,0:T(8,128)(2,1)} %bitcast.12, bf16[256,256]{1,0:T(8,128)(2,1)} %bitcast.14, ...), custom_call_target="tpu_custom_call" | custom-call | tf_op jit(solution)/shard_map/fused_solve/pallas_call | solution.py:612
  91.1 3.0 %place_results.1 = (bf16[256,1024]{1,0:T(8,128)(2,1)}, bf16[256,1024]{1,0:T(8,128)(2,1)}, bf16[5,256,1024]{2,1,0:T(8,128)(2,1)}) custom-call(bf16[256,1024]{1,0:T(8,128)(2,1)} %get-tuple-element.9.leaf_in, bf16[256,1024]{1,0:T(8,128)(2,1)} %get-tuple-element.10.mid_in, bf16[5,256,1024]{2,1,0:T(8,128)(2,1)} %get-tuple-element.11.anc_in), custom_call_target="tpu_custom_call" | custom-call | tf_op jit(solution)/shard_map/place_results/pallas_call | solution.py:682

commit v3 on v2

--- a/solution.py
+++ b/solution.py
@@ -253,11 +253,17 @@
 
     lax.fori_loop(0, plane, leaf_step, 0)
 
+    first = ancestors // 2
+
+    def block_ref(which, kind):
+        part = {5: slice(0, first), 6: slice(first, ancestors)}.get(kind, slice(0, ancestors))
+        return ancb.at[part, :, depth_of(which)]
+
     def block_copy(kind):
-        which = (me, me, me, slot(other, row), slot(layer, far_row), slot(layer, far_row))
-        which = (which + (slot(other, far_row),))[kind]
-        to = (sib, across, far, sib, sib, across, sib)[kind]
-        ref = ancb.at[:, :, depth_of(which)]
+        beside, beyond = slot(other, row), slot(layer, far_row)
+        which = (me, me, me, beside, beyond, beyond, beside, slot(other, far_row))[kind]
+        to = (sib, across, far, sib, sib, across, far, sib)[kind]
+        ref = block_ref(which, kind)
         return remote(ref, ref, g_send.at[kind], g_recv.at[kind], to)
 
     def block_arrival(kind):
@@ -268,9 +274,10 @@
             slot(other, sib_row),
             slot(layer, far_sib_row),
             slot(other, far_row),
+            slot(other, far_row),
             slot(other, far_sib_row),
         )[kind]
-        ref = ancb.at[:, :, depth_of(which)]
+        ref = block_ref(which, kind)
         return remote(ref, ref, g_send.at[kind], g_recv.at[kind], sib)
 
     loads[2].wait()
@@ -337,7 +344,9 @@
     loads[4].wait()
     loads[5].wait()
     forward_leaf(0)
-    lag = jnp.where((col == 0) | (col == cols - 1), LAG_END, LAG_INSIDE)
+    at_end = (col == 0) | (col == cols - 1)
+    lag = jnp.where(at_end, LAG_END, LAG_INSIDE)
+    relay_at = jnp.where(at_end, 6, 5)
 
     def sum_step(j, carry):
         @pl.when(j < plane)
@@ -367,13 +376,20 @@
         @pl.when(j == 3)
         def _():
             block_arrival(1).wait_recv()
+            block_copy(6).start()
             block_copy(3).start()
 
-        @pl.when(j == 6)
+        @pl.when(j == relay_at)
         def _():
             block_arrival(2).wait_recv()
             block_copy(5).start()
             block_copy(4).start()
+
+        @pl.when(j == plane)
+        def _():
+            block_arrival(5).wait_recv()
+            block_arrival(6).wait_recv()
+            block_copy(7).start()
 
         @pl.when((j >= lag) & (j < plane + lag))
         def _():
@@ -409,9 +425,7 @@
 
     lax.fori_loop(0, plane + max(LAG_END, LAG_INSIDE), sum_step, 0)
 
-    block_arrival(5).wait_recv()
-    block_copy(6).start()
-    for kind in (0, 3, 4, 6):
+    for kind in (0, 3, 4, 7):
         block_arrival(kind).wait_recv()
     for step in range(1, plane):
         peer = (me + step) % plane
@@ -550,7 +564,7 @@
         return carry
 
     lax.fori_loop(0, plane, drain, 0)
-    for kind in range(7):
+    for kind in range(8):
         block_copy(kind).wait_send()
     for a in range(ancestors):
         up_copy(a, part_inner, 1, sib).wait_send()
@@ -654,8 +668,8 @@
             dma((2, plane, cols)),
             dma((plane,)),
             dma((plane,)),
-            dma((7,)),
-            dma((7,)),
+            dma((8,)),
+            dma((8,)),
             dma((2, ancestors)),
             dma((2, ancestors)),
             dma((7, ancestors)),
@@ -697,9 +711,9 @@
     return (leaf_sol[None, None, None, None], mid_sol[None, None, None], anc_sol)
 
 
-def fits_fused(mesh, rhs_count):
+def fits_fused(mesh, rhs_count, ancestors):
     layers, rows, cols = (mesh.shape[name] for name in ("layer", "row", "col"))
-    pairs = layers == 2 and rows == 4 and cols % 2 == 0
+    pairs = layers == 2 and rows == 4 and cols % 2 == 0 and ancestors > 1
     return pairs and rhs_count % (layers * rows * 128) == 0
 
 
@@ -726,7 +740,7 @@
 
     def run(leaf_rhs, *rest):
         chosen = body
-        if fits_fused(mesh, leaf_rhs.shape[-1]) and leaf_rhs.shape[3] == 1:
+        if fits_fused(mesh, leaf_rhs.shape[-1], rest[-2].shape[0]) and leaf_rhs.shape[3] == 1:
             sizes = (mesh.shape[name] for name in ("layer", "row", "col"))
             chosen = functools.partial(fused_body, *sizes)
         return jax.shard_map(

time: 94.3 us -> 88.6 us (0.940)
  Pallas kernels: 92.8 us -> 87.1 us
    pallas_call x1, Pallas kernels: 89.8 us -> 84.1 us  [fused_body(): pl.pallas_call(functools.partial(fused_kernel, layers, rows, cols), out_s...]
where the time goes in v3:
time: 88.6 us; the launch traced here: 88.4 us
  Pallas kernels  87.1 us (98%)
  between operations  1.29 us (1%)
    pallas_call x1, Pallas kernels, fused_body(): pl.pallas_call(functools.partial(fused_kernel, layers, rows, cols), out_s...  84.1 us
    pallas_call x1, Pallas kernels, fused_body(): pl.pallas_call(place_results, out_shape=[jax.ShapeDtypeStruct(value.shape...  3.02 us

profile of v3, /device:TPU:0, one launch (start us, length us, event | category | flops | bytes accessed | tf_op | source)
XLA Modules:
  0.0 88.4 jit_solution(14669435281212335942)
XLA Ops:
  1.3 84.1 %fused_solve.1 = (bf16[256,1024]{1,0:T(8,128)(2,1)}, bf16[256,1024]{1,0:T(8,128)(2,1)}, bf16[5,256,1024]{2,1,0:T(8,128)(2,1)}) custom-call(s32[16]{0:T(128)} %bitcast.16, s32[16]{0:T(128)} %bitcast.17, s32[1,1,1]{2,1,0:T(1,128)S(6)} %copy.15.block_count_h, bf16[256,1024]{1,0:T(8,128)(2,1)} %bitcast.12, bf16[256,256]{1,0:T(8,128)(2,1)} %bitcast.14, ...), custom_call_target="tpu_custom_call" | custom-call | tf_op jit(solution)/shard_map/fused_solve/pallas_call | solution.py:626
  85.4 3.0 %place_results.1 = (bf16[256,1024]{1,0:T(8,128)(2,1)}, bf16[256,1024]{1,0:T(8,128)(2,1)}, bf16[5,256,1024]{2,1,0:T(8,128)(2,1)}) custom-call(bf16[256,1024]{1,0:T(8,128)(2,1)} %get-tuple-element.9.leaf_in, bf16[256,1024]{1,0:T(8,128)(2,1)} %get-tuple-element.10.mid_in, bf16[5,256,1024]{2,1,0:T(8,128)(2,1)} %get-tuple-element.11.anc_in), custom_call_target="tpu_custom_call" | custom-call | tf_op jit(solution)/shard_map/place_results/pallas_call | solution.py:696

commit v4 on v3

--- a/solution.py
+++ b/solution.py
@@ -534,11 +534,12 @@
             sum_up(a)
         if a >= 2:
             total_down(a - 2, True)
-    for a in range(ancestors):
-        total_down(a, False)
-        solve(a)
-    for a in range(ancestors):
-        relay(a)
+    for a in range(ancestors + 2):
+        if a < ancestors:
+            total_down(a, False)
+            solve(a)
+        if a >= 2:
+            relay(a - 2)
     for a in range(ancestors):
         sol_arrival(a, 5).wait_recv()
         sol_copy(a, 6).start()

time: 88.6 us -> 90 us (1.016)
  Pallas kernels: 87.1 us -> 88.6 us
    pallas_call x1, Pallas kernels: 84.1 us -> 85.5 us  [fused_body(): pl.pallas_call(functools.partial(fused_kernel, layers, rows, cols), out_s...]
where the time goes in v4:
time: 90 us; the launch traced here: 89.9 us
  Pallas kernels  88.6 us (98%)
  between operations  1.29 us (1%)
    pallas_call x1, Pallas kernels, fused_body(): pl.pallas_call(functools.partial(fused_kernel, layers, rows, cols), out_s...  85.5 us
    pallas_call x1, Pallas kernels, fused_body(): pl.pallas_call(place_results, out_shape=[jax.ShapeDtypeStruct(value.shape...  3.02 us

profile of v4, /device:TPU:0, one launch (start us, length us, event | category | flops | bytes accessed | tf_op | source)
XLA Modules:
  0.0 89.9 jit_solution(16861976010337109134)
XLA Ops:
  1.3 85.5 %fused_solve.1 = (bf16[256,1024]{1,0:T(8,128)(2,1)}, bf16[256,1024]{1,0:T(8,128)(2,1)}, bf16[5,256,1024]{2,1,0:T(8,128)(2,1)}) custom-call(s32[16]{0:T(128)} %bitcast.16, s32[16]{0:T(128)} %bitcast.17, s32[1,1,1]{2,1,0:T(1,128)S(6)} %copy.15.block_count_h, bf16[256,1024]{1,0:T(8,128)(2,1)} %bitcast.12, bf16[256,256]{1,0:T(8,128)(2,1)} %bitcast.14, ...), custom_call_target="tpu_custom_call" | custom-call | tf_op jit(solution)/shard_map/fused_solve/pallas_call | solution.py:627
  86.8 3.0 %place_results.1 = (bf16[256,1024]{1,0:T(8,128)(2,1)}, bf16[256,1024]{1,0:T(8,128)(2,1)}, bf16[5,256,1024]{2,1,0:T(8,128)(2,1)}) custom-call(bf16[256,1024]{1,0:T(8,128)(2,1)} %get-tuple-element.9.leaf_in, bf16[256,1024]{1,0:T(8,128)(2,1)} %get-tuple-element.10.mid_in, bf16[5,256,1024]{2,1,0:T(8,128)(2,1)} %get-tuple-element.11.anc_in), custom_call_target="tpu_custom_call" | custom-call | tf_op jit(solution)/shard_map/place_results/pallas_call | solution.py:697
